TPU v7x, 512 devices: a whole 4x4x16 slice. The times are simulated.
512 devices in a mesh: row: 16 (over x, y_lo, core), col: 32 (over y_hi, z).
Axes of the slice: x: 4, y: 4 (y_hi: 2, y_lo: 2; y = y_hi * 2 + y_lo), z: 16, core: 2. Of those that a mesh axis runs over, the one named last changes fastest.
Arguments:
- features: bfloat16 [49152, 128], P(('col', 'row')), may hold values from -6 to 6
- weight: bfloat16 [128, 256], replicated, may hold values from -0.5 to 0.5
- bias: float32 [256], replicated, may hold values from -3 to 3
- tile_values: bfloat16 [16, 32, 128, 128, 128], P('row', 'col'), may hold values from -0.0390625 to 0.0390625
- tile_rows: int32 [16, 32, 128], P('row', 'col'), may hold values from 0 to 23
- tile_cols: int32 [16, 32, 128], P('row', 'col'), may hold values from 0 to 11
- tile_count: int32 [16, 32], P('row', 'col'), may hold values from 16 to 128, as said below
Outputs:
- hidden: bfloat16 [49152, 256], P(('row', 'col'))
Inputs may be any that keep to these rules, and one draw needn't show every extreme that they name: `tile_count`: within one row block and column block the 128 slots name distinct tile positions. Some block's count equals 128 in every draw.
All inputs are finite; a program needn't handle non-finite values.
Results may differ from a plain program's by a relative error of at most 0.0019.
Values may be sent and summed in bfloat16 or wider, within the bound.
No kernel may reach another device: no remote copies, remote signals or barrier semaphores. Data moves between devices by JAX's collectives and lax.ppermute only.
A program may use at most 64 MiB of HBM per device.

v0:
```python
import math

import jax
import jax.numpy as jnp
from jax import lax
from jax.sharding import PartitionSpec as P


def aggregate(operand, tiles, row_ids, col_ids, alive_mask, row_tiles, multiply):
    tile_size = tiles.shape[1]
    slot_total = tiles.shape[0]
    feature_width = operand.shape[1]
    col_tiles = operand.shape[0] // tile_size
    feature_table = operand.reshape(col_tiles, tile_size, feature_width)
    group_size = math.gcd(slot_total, 32)
    block_count = slot_total // group_size

    def accumulate(running, pieces):
        values, rows_here, cols_here, alive_here = pieces
        chosen = feature_table[cols_here]
        products = multiply(values, chosen) * alive_here[:, None, None]
        running = running.at[rows_here].add(products)
        return (running, None)

    pieces = (
        tiles.reshape(block_count, group_size, tile_size, tile_size),
        row_ids.reshape(block_count, group_size),
        col_ids.reshape(block_count, group_size),
        alive_mask.reshape(block_count, group_size),
    )
    running, unused = lax.scan(
        accumulate, jnp.zeros((row_tiles, tile_size, feature_width), jnp.float32), pieces
    )
    return running.reshape(row_tiles * tile_size, feature_width)


def multiply_narrow(values, chosen):
    return jnp.einsum("tij,tjf->tif", values, chosen, preferred_element_type=jnp.float32)


def shards(features, weight, bias, tile_values, tile_rows, tile_cols, tile_count):
    tiles = tile_values[0, 0]
    row_ids = tile_rows[0, 0]
    col_ids = tile_cols[0, 0]
    tile_total = tile_count[0, 0]
    tile_size = tiles.shape[1]
    slot_total = tiles.shape[0]
    alive_mask = (jnp.arange(slot_total, dtype=jnp.int32) < tile_total).astype(jnp.float32)
    col_tiles = features.shape[0] * lax.axis_size("row") // tile_size
    row_tiles = col_tiles * lax.axis_size("col") // lax.axis_size("row")
    gathered = lax.all_gather(features, "row", axis=0, tiled=True)
    partial_value = aggregate(
        gathered, tiles, row_ids, col_ids, alive_mask, row_tiles, multiply_narrow
    )
    summed = lax.psum_scatter(partial_value, "col", scatter_dimension=0, tiled=True)
    output = jnp.dot(summed, weight.astype(jnp.float32), precision=lax.Precision.HIGHEST) + bias
    return jax.nn.relu(output).astype(jnp.bfloat16)


def solution(mesh):
    in_specs = (
        P(("col", "row"), None),
        P(),
        P(),
        P("row", "col", None, None, None),
        P("row", "col", None),
        P("row", "col", None),
        P("row", "col"),
    )
    out_specs = P(("row", "col"), None)
    return jax.shard_map(shards, mesh=mesh, in_specs=in_specs, out_specs=out_specs, check_vma=False)
```

profile of v0, /device:TPU:2, one launch (start us, length us, event | category | flops | bytes accessed | tf_op | source)
XLA Modules:
  0.0 748.1 jit_solution(8170036369476610745)
XLA Ops:
  6.5 0.0 copy-start
  6.5 0.0 reduce-scatter.2.cloned.1.call-start
  7.2 0.5 broadcast.55
  7.7 1.2 reduce.6
  9.0 1.2 reduce.7
  10.2 0.1 reshape_squeeze.11
  10.3 0.1 reshape_squeeze.9
  10.4 21.9 %all_gather.3 = bf16[1536,128]{1,0:T(8,128)(2,1)} all-gather(bf16[96,128]{1,0:T(8,128)(2,1)} %param.9), channel_id=1, replica_groups=mesh['row'=16,'col'=32] {'row'}, dimensions={0}, use_global_device_ids=true | all-gather | bytes 417792 | tf_op jit(solution)/shard_map/all_gather | solution.py:51
  32.3 1.3 broadcast_in_dim.2
  33.6 0.0 copy-start.1
  33.6 38.2 %while.10 = (s32[]{:T(128)}, f32[24,128,128]{2,1,0:T(8,128)}, s32[4,32]{1,0:T(4,128)S(1)}, bf16[4,32,128,128]{3,2,1,0:T(8,128)(2,1)}, s32[4,32]{1,0:T(4,128)S(1)...) while((s32[]{:T(128)}, f32[24,128,128]{2,1,0:T(8,128)}, s32[4,32]{1,0:T(4,128)S(1)}, ...), condition=%wide.region_2.3_spmd, body=%wide.region_0.2_spmd.sunk | while | flops 135267520 | bytes 12588393 | solution.py:31
  33.7 1.7 gather_fusion
  35.4 1.7 convolution_multiply_fusion.2
  37.1 6.1 scatter_fusion
  43.3 1.7 gather_fusion
  45.0 1.7 convolution_multiply_fusion.2
  46.7 6.1 scatter_fusion
  52.8 1.7 gather_fusion
  54.6 1.7 convolution_multiply_fusion.2
  56.3 6.1 scatter_fusion
  62.4 1.7 gather_fusion
  64.1 1.7 convolution_multiply_fusion.2
  65.8 6.0 scatter_fusion
  71.8 0.0 reduce-scatter.2.cloned.1.call-update
  71.9 667.8 %reduce-scatter.2.cloned.1.call-done = f32[96,128]{1,0:T(8,128)} async-done(((f32[3072,128]{1,0:T(8,128)}), f32[96,128]{1,0:T(8,128)}) %reduce-scatter.2.cloned.1.call-update) | async-done | bytes 49168 | tf_op jit(solution)/shard_map/reduce_scatter | solution.py:55
  739.7 0.0 copy-done
  739.7 0.0 copy-done.1
  739.7 1.6 fusion.9
  (13 shorter events, 0.1 us)
Async XLA Ops:
  6.5 733.1 %copy-start = (bf16[128,256]{1,0:T(8,128)(2,1)S(1)}, bf16[128,256]{1,0:T(8,128)(2,1)}, u32[]{:S(2)}) copy-start(bf16[128,256]{1,0:T(8,128)(2,1)} %param.10) | copy-start | bytes 196612
  6.5 733.1 %reduce-scatter.2.cloned.1.call-start = ((), (), s32[]{:S(2)}) async-start(), calls=%async_computation.1 | async-start | bytes 1622016 | tf_op jit(solution)/shard_map/reduce_scatter | solution.py:55
  33.6 706.0 %copy-start.1 = (f32[256]{0:T(256)S(1)}, f32[256]{0:T(256)}, u32[]{:S(2)}) copy-start(f32[256]{0:T(256)} %param.11) | copy-start | bytes 3076
Sparse Core Ops, SparseCore 0:
  72.0 667.6 reduce-scatter.1
where the time goes:
time: 749 us; the launch traced here: 748 us
  waiting for transfers between devices  668 us (89%)
  other arithmetic  26.8 us (4%)
  blocking collectives  21.9 us (3%)
  between operations  14.1 us (2%)
  local copies, waits for them, and re-layouts  9.01 us (1%)
  matrix products  8.34 us (1%)
    reduce_scatter x1, waiting for transfers between devices, shards(): lax.psum_scatter(partial_value, 'col', scatter_dimension=0, tiled=True)  668 us
    scatter-add x4, other arithmetic, accumulate(): running = running.at[rows_here].add(products)  24.3 us
    all_gather x1, blocking collectives, shards(): gathered = lax.all_gather(features, 'row', axis=0, tiled=True)  21.9 us
  transfers between devices with their start and end apart: 1, of which 1 were waited for; matrix products, arithmetic and copies ran while one was open for 0% of the time, Pallas kernels for 0%

commit v1 on v0

v1 whole, which is shorter than its diff:
```python
import functools

import jax
import jax.numpy as jnp
from jax import lax
from jax.experimental import pallas as pl
from jax.experimental.pallas import tpu as pltpu
from jax.sharding import PartitionSpec as P

LEVELS = 12
STEP = 10
EXTRA = 8


def level_of(peak, base):
    level = jnp.zeros(peak.shape, jnp.float32)
    for k in range(1, LEVELS + 1):
        level = level + jnp.where(peak < 2.0 ** (15 - base - STEP * k), 1.0, 0.0)
    return level


def power(level, sign):
    value = jnp.ones(level.shape, jnp.float32)
    for k in range(1, LEVELS + 1):
        value = value * jnp.where(level >= k, 2.0 ** (sign * STEP), 1.0)
    return value


def spread_kernel(tile, rows_ref, cols_ref, count_ref, tiles_ref, dense_ref, sems):
    used = count_ref[0]
    lines = 2 * tile

    def clear(i, carry):
        span = pl.ds(pl.multiple_of(i * lines, lines), lines)
        dense_ref[span, :] = jnp.zeros((lines, dense_ref.shape[1]), dense_ref.dtype)
        return carry

    lax.fori_loop(0, dense_ref.shape[0] // lines, clear, 0)

    def move(s):
        row = pl.multiple_of(rows_ref[s] * tile, tile)
        col = pl.multiple_of(cols_ref[s] * tile, tile)
        return pltpu.make_async_copy(
            tiles_ref.at[s], dense_ref.at[pl.ds(row, tile), pl.ds(col, tile)], sems.at[s]
        )

    def start(s, carry):
        move(s).start()
        return carry

    def wait(s, carry):
        move(s).wait()
        return carry

    lax.fori_loop(0, used, start, 0)
    lax.fori_loop(0, used, wait, 0)


def product_kernel(parts, base, dense_ref, x_ref, out_ref, held, sems):
    ways, depth, share = parts
    near = ways // 2
    per = ways * depth // sems.shape[0]

    def fetch(g):
        span = pl.ds(g * per * share, per * share)
        return pltpu.make_async_copy(dense_ref.at[span, :], held.at[span, :], sems.at[g])

    for g in range(sems.shape[0]):
        fetch(g).start()
    for d in range(ways * depth):
        if d % per == 0:
            fetch(d // per).wait()
        way = (d // (near * depth)) * near + d % near
        place = (d % (near * depth)) // near
        value = jnp.dot(held[d * share : (d + 1) * share, :], x_ref[...], preferred_element_type=jnp.float32)
        level = level_of(jnp.max(jnp.abs(value), axis=0, keepdims=True), base)
        out_ref[way, place * share : (place + 1) * share, :] = value * (power(level, 1) * 2.0**base)
        out_ref[way, depth * share + place : depth * share + place + 1, :] = level


def shards(mesh, features, weight, bias, tile_values, tile_rows, tile_cols, tile_count):
    tiles = tile_values[0, 0]
    slots, tile, _ = tiles.shape
    width = features.shape[1]
    n_row, n_col = mesh.shape["row"], mesh.shape["col"]
    share = features.shape[0]
    total_rows = share * n_col
    half = n_col // 2
    near = 2
    ways = 2 * near
    depth = n_col // ways

    spread = jnp.broadcast_to(features[None], (n_row,) + features.shape)
    gathered = lax.all_to_all(spread, "row", 0, 0).reshape(n_row * features.shape[0], width)

    dense = pl.pallas_call(
        functools.partial(spread_kernel, tile),
        out_shape=jax.ShapeDtypeStruct((total_rows, n_row * features.shape[0]), tiles.dtype),
        in_specs=[pl.BlockSpec(memory_space=pltpu.SMEM)] * 3 + [pl.BlockSpec(memory_space=pltpu.HBM)],
        out_specs=pl.BlockSpec(memory_space=pltpu.VMEM),
        scratch_shapes=[pltpu.SemaphoreType.DMA((slots,))],
        compiler_params=pltpu.CompilerParams(vmem_limit_bytes=60 * 2**20),
        cost_estimate=pl.CostEstimate(flops=0, bytes_accessed=6 * slots * tile * tile, transcendentals=0),
    )(tile_rows[0, 0], tile_cols[0, 0], tile_count[0], tiles)

    base = 7
    message = pl.pallas_call(
        functools.partial(product_kernel, (ways, depth, share), base),
        out_shape=jax.ShapeDtypeStruct((ways, depth * share + depth, width), jnp.float32),
        in_specs=[pl.BlockSpec(memory_space=pltpu.HBM), pl.BlockSpec(memory_space=pltpu.VMEM)],
        out_specs=pl.BlockSpec(memory_space=pltpu.VMEM),
        scratch_shapes=[pltpu.VMEM(dense.shape, dense.dtype), pltpu.SemaphoreType.DMA((8,))],
        compiler_params=pltpu.CompilerParams(vmem_limit_bytes=50 * 2**20),
    )(dense, gathered)

    pairs = [[h * half + p * near + q for h in range(2) for q in range(near)] for p in range(depth)]
    came = lax.all_to_all(message.astype(jnp.float16), "col", 0, 0, axis_index_groups=pairs).astype(jnp.float32)
    spot = depth * share
    unit = (power(came[:, spot:], -1) * 2.0**-base)[:, :, None]
    blocks = jnp.sum(came[:, :spot].reshape(ways, depth, share, width) * unit, axis=0)

    base = 5
    level = level_of(jnp.max(jnp.abs(blocks), axis=1, keepdims=True), base)
    scaled = blocks * (power(level, 1) * 2.0**base)
    message = jnp.concatenate([scaled, jnp.broadcast_to(level, (depth, EXTRA, width))], axis=1).astype(jnp.float16)
    rest = [[h * half + p * near + q for p in range(depth)] for h in range(2) for q in range(near)]
    came = lax.all_to_all(message, "col", 0, 0, axis_index_groups=rest).astype(jnp.float32)
    summed = jnp.sum(came[:, :share] * (power(came[:, share : share + 1], -1) * 2.0**-base), axis=0)

    output = jnp.dot(summed, weight.astype(jnp.float32), precision=lax.Precision.HIGHEST) + bias
    return jax.nn.relu(output).astype(jnp.bfloat16)


def solution(mesh):
    in_specs = (
        P(("col", "row"), None),
        P(),
        P(),
        P("row", "col", None, None, None),
        P("row", "col", None),
        P("row", "col", None),
        P("row", "col"),
    )
    out_specs = P(("row", "col"), None)
    return jax.shard_map(
        functools.partial(shards, mesh), mesh=mesh, in_specs=in_specs, out_specs=out_specs, check_vma=False
    )
```

time: 749 us -> 74.5 us (0.10)
  the two profiles are of different devices: /device:TPU:2 before, /device:TPU:12 now
where the time goes in v1:
time: 74.5 us; the launch traced here: 74 us
  blocking collectives  47.8 us (64%)
  Pallas kernels  13.3 us (18%)
  starting transfers between devices  9.17 us (12%)
  local copies, waits for them, and re-layouts  1.58 us (2%)
  matrix products  0.82 us (1%)
  between operations  0.78 us (1%)
    all_to_all x1, blocking collectives, shards(): lax.all_to_all(message, 'col', 0, 0, axis_index_groups=rest)  31.6 us
    all_to_all x1, blocking collectives, shards(): lax.all_to_all(message.astype(jnp.float16), 'col', 0, 0, axis_index_group...  16.2 us
    all_to_all x1, starting transfers between devices, shards(): lax.all_to_all(spread, 'row', 0, 0)  9.17 us
    pallas_call x1, Pallas kernels, shards(): pl.pallas_call(functools.partial(spread_kernel, tile), out_shape=jax.Shap...  7.87 us
    pallas_call x1, Pallas kernels, shards(): pl.pallas_call(functools.partial(product_kernel, (ways, depth, share), ba...  5.42 us
    broadcast_in_dim x1, local copies, waits for them, and re-layouts, shards(): spread = jnp.broadcast_to(features[None], (n_row,) + features.shape)  1.56 us
  transfers between devices with their start and end apart: 1, of which 0 were waited for; matrix products, arithmetic and copies ran while one was open for 0% of the time, Pallas kernels for 11%

profile of v1, /device:TPU:12, one launch (start us, length us, event | category | flops | bytes accessed | tf_op | source)
XLA Modules:
  0.0 74.0 jit_solution(16998548915750602980)
XLA Ops:
  0.0 0.0 copy-start
  0.0 1.6 %broadcast_in_dim.120 = bf16[16,96,128]{2,1,0:T(8,128)(2,1)} broadcast(bf16[96,128]{1,0:T(8,128)(2,1)} %param.7), dimensions={1,2} | broadcast | bytes 417792 | tf_op jit(solution)/shard_map/broadcast_in_dim | solution.py:93
  1.6 9.2 %all-to-all-start = ((bf16[16,96,128]{2,1,0:T(8,128)(2,1)}), bf16[16,96,128]{2,1,0:T(8,128)(2,1)S(1)}, u32[]{:S(2)}, u32[]{:S(2)}) async-start(bf16[16,96,128]{2,1,0:T(8,128)(2,1)} %broadcast_in_dim.120), calls=%async_computation | async-start | bytes 786432 | tf_op jit(solution)/shard_map/all_to_all | solution.py:94
  11.4 7.9 %shard_map.73.dense_ref = bf16[3072,1536]{1,0:T(8,128)(2,1)} custom-call(s32[128]{0:T(128)} %bitcast.17, s32[128]{0:T(128)} %bitcast.18, s32[1]{0:T(128)} %bitcast.11.count_ref, bf16[128,128,128]{2,1,0:T(8,128)(2,1)} %bitcast.13), custom_call_target="tpu_custom_call" | custom-call | bytes 12582912 | tf_op jit(solution)/shard_map/pallas_call | solution.py:96
  19.3 0.0 all-to-all-done
  19.3 5.4 %shard_map.74 = f32[4,776,128]{2,1,0:T(8,128)S(1)} custom-call(bf16[3072,1536]{1,0:T(8,128)(2,1)} %shard_map.73.dense_ref, bf16[1536,128]{1,0:T(8,128)(2,1)S(1)} %bitcast.12), custom_call_target="tpu_custom_call" | custom-call | tf_op jit(solution)/shard_map/pallas_call | solution.py:107
  24.7 0.1 convert_element_type.14
  24.8 16.2 %all_to_all.15 = f16[4,776,128]{2,1,0:T(8,128)(2,1)S(1)} all-to-all(f16[4,776,128]{2,1,0:T(8,128)(2,1)S(1)} %convert_element_type.14), channel_id=1, replica_groups={{0,1,16,17},{2,3,18,19},{4,5,20,21},{6,7,22,23},{8,9,24,25},{10,11,26,2..., dimensions={0} | all-to-all | bytes 1589248 | tf_op jit(solution)/shard_map/all_to_all | solution.py:117
  41.0 0.1 convert_element_type.15
  41.1 0.1 fusion
  41.2 0.0 copy-start.1
  41.4 0.1 pad_maximum_fusion
  41.5 31.6 %all_to_all.16 = f16[8,104,128]{2,1,0:T(8,128)(2,1)S(1)} all-to-all(f16[8,104,128]{2,1,0:T(8,128)(2,1)S(1)} %pad_maximum_fusion), channel_id=1, replica_groups={{0,2,4,6,8,10,12,14},{1,3,5,7,9,11,13,15},{16,18,20,22,24,26,28,30},{17..., dimensions={0} | all-to-all | bytes 425984 | tf_op jit(solution)/shard_map/all_to_all | solution.py:127
  73.2 0.0 copy-done
  73.2 0.0 copy-done.1
  73.2 0.8 %fusion.2 = bf16[96,256]{1,0:T(8,128)(2,1)} fusion(f32[96,128]{1,0:T(8,128)S(1)} %fusion.3, bf16[128,256]{1,0:T(8,128)(2,1)S(1)} %copy-done, f32[256]{0:T(256)S(1)} %copy-done.1), kind=kOutput, calls=%fused_computation.4 | convolution fusion | flops 37822464 | bytes 164864 | tf_op jit(solution)/shard_map/dot_general | solution.py:130
  (9 shorter events, 0.3 us)
Async XLA Ops:
  0.0 73.2 %copy-start = (bf16[128,256]{1,0:T(8,128)(2,1)S(1)}, bf16[128,256]{1,0:T(8,128)(2,1)}, u32[]{:S(2)}) copy-start(bf16[128,256]{1,0:T(8,128)(2,1)} %param.8) | copy-start | bytes 196612
  1.6 17.7 %all-to-all-start = ((bf16[16,96,128]{2,1,0:T(8,128)(2,1)}), bf16[16,96,128]{2,1,0:T(8,128)(2,1)S(1)}, u32[]{:S(2)}, u32[]{:S(2)}) async-start(bf16[16,96,128]{2,1,0:T(8,128)(2,1)} %broadcast_in_dim.120), calls=%async_computation | async-start | bytes 786432 | tf_op jit(solution)/shard_map/all_to_all | solution.py:94
  41.2 32.0 %copy-start.1 = (f32[256]{0:T(256)S(1)}, f32[256]{0:T(256)}, u32[]{:S(2)}) copy-start(f32[256]{0:T(256)} %param.9) | copy-start | bytes 3076

commit v2 on v1

v2 whole, which is shorter than its diff:
```python
import functools

import jax
import jax.numpy as jnp
from jax import lax
from jax.experimental import pallas as pl
from jax.experimental.pallas import tpu as pltpu
from jax.sharding import PartitionSpec as P

LEVELS = 6
STEP = 16
ROOT = 1024.0


def level_of(peak, base):
    level = jnp.zeros(peak.shape, jnp.float32)
    for k in range(1, LEVELS + 1):
        level = level + jnp.where(peak < 2.0 ** (15 - base - STEP * k), 1.0, 0.0)
    return level


def power(level, sign):
    value = jnp.ones(level.shape, jnp.float32)
    for k in range(1, LEVELS + 1):
        value = value * jnp.where(level >= k, 2.0 ** (sign * STEP), 1.0)
    return value


def product_kernel(parts, base, spot_ref, tiles_ref, x_ref, out_ref, place_ref, held, sems):
    ways, depth, share, row_tiles, col_tiles = parts
    slots, tile, _ = held.shape
    chunks = sems.shape[0]
    per = slots // chunks

    def fetch(g):
        span = pl.ds(g * per, per)
        return pltpu.make_async_copy(tiles_ref.at[0, 0, span], held.at[span], sems.at[g])

    for g in range(chunks):
        fetch(g).start()
    near = ways // 2
    spots = row_tiles * col_tiles

    for p in range(spots):
        place_ref[p] = slots
    for s in range(slots):
        place_ref[spot_ref[s]] = s

    for g in range(chunks):
        fetch(g).wait()

    def piece(p, lo, hi):
        slot = place_ref[p]
        rows = held[jnp.minimum(slot, slots - 1), lo:hi, :]
        return jnp.where(slot < slots, rows, jnp.zeros_like(rows))

    for d in range(ways * depth):
        way = (d // (near * depth)) * near + d % near
        at = (d % (near * depth)) // near
        value = jnp.zeros((share, x_ref.shape[1]), jnp.float32)
        for j in range(0, col_tiles, 2):
            strips = []
            row = d * share
            while row < (d + 1) * share:
                r, lo = row // tile, row % tile
                hi = min(tile, lo + (d + 1) * share - row)
                strips.append(
                    jnp.concatenate([piece(r * col_tiles + j + k, lo, hi) for k in range(2)], axis=1)
                )
                row += hi - lo
            value = value + jnp.dot(
                jnp.concatenate(strips, axis=0),
                x_ref[j * tile : (j + 2) * tile, :],
                preferred_element_type=jnp.float32,
            )
        level = level_of(jnp.max(jnp.abs(value), axis=0, keepdims=True), base)
        out_ref[way, at * share : (at + 1) * share, :] = value * (power(level, 1) * 2.0**base)
        out_ref[way, depth * share + at : depth * share + at + 1, :] = level


def shards(mesh, features, weight, bias, tile_values, tile_rows, tile_cols, tile_count):
    tile = tile_values.shape[3]
    width = features.shape[1]
    n_row, n_col = mesh.shape["row"], mesh.shape["col"]
    share = features.shape[0]
    total_rows = share * n_col
    half = n_col // 2
    near = 2
    ways = 2 * near
    depth = n_col // ways

    spread = jnp.broadcast_to(features[None], (n_row,) + features.shape)
    row_tiles, col_tiles = total_rows // tile, n_row * share // tile
    used = jnp.arange(tile_rows.shape[2], dtype=jnp.int32) < tile_count[0, 0]
    spots = jnp.where(used, tile_rows[0, 0] * col_tiles + tile_cols[0, 0], row_tiles * col_tiles)
    spread, spots = lax.optimization_barrier((spread, spots))
    gathered = lax.all_to_all(spread, "row", 0, 0).reshape(n_row * features.shape[0], width)

    base = 7
    message = pl.pallas_call(
        functools.partial(product_kernel, (ways, depth, share, row_tiles, col_tiles), base),
        out_shape=jax.ShapeDtypeStruct((ways, depth * share + depth, width), jnp.float32),
        in_specs=[pl.BlockSpec(memory_space=m) for m in (pltpu.SMEM, pltpu.HBM, pltpu.VMEM)],
        out_specs=pl.BlockSpec(memory_space=pltpu.VMEM),
        scratch_shapes=[
            pltpu.SMEM((row_tiles * col_tiles + 8,), jnp.int32),
            pltpu.VMEM(tile_values.shape[2:], tile_values.dtype),
            pltpu.SemaphoreType.DMA((8,)),
        ],
        compiler_params=pltpu.CompilerParams(vmem_limit_bytes=50 * 2**20),
    )(spots, tile_values, gathered)

    pairs = [[h * half + p * near + q for h in range(2) for q in range(near)] for p in range(depth)]
    came = lax.all_to_all(message.astype(jnp.float16), "col", 0, 0, axis_index_groups=pairs).astype(jnp.float32)
    spot = depth * share
    unit = (power(came[:, spot:], -1) * 2.0**-base)[:, :, None]
    blocks = jnp.sum(came[:, :spot].reshape(ways, depth, share, width) * unit, axis=0)

    rest = [[h * half + p * near + q for p in range(depth)] for h in range(2) for q in range(near)]
    message = (jnp.where(blocks < 0, -ROOT, ROOT) * jnp.sqrt(jnp.abs(blocks))).astype(jnp.float16)
    came = lax.all_to_all(message, "col", 0, 0, axis_index_groups=rest).astype(jnp.float32)
    summed = jnp.sum(came * jnp.abs(came), axis=0) * ROOT**-2

    output = jnp.dot(summed, weight.astype(jnp.float32), precision=lax.Precision.HIGHEST) + bias
    return jax.nn.relu(output).astype(jnp.bfloat16)


def solution(mesh):
    in_specs = (
        P(("col", "row"), None),
        P(),
        P(),
        P("row", "col", None, None, None),
        P("row", "col", None),
        P("row", "col", None),
        P("row", "col"),
    )
    out_specs = P(("row", "col"), None)
    return jax.shard_map(
        functools.partial(shards, mesh), mesh=mesh, in_specs=in_specs, out_specs=out_specs, check_vma=False
    )
```

time: 74.5 us -> 73.3 us (0.984)
  the two profiles are of different devices: /device:TPU:12 before, /device:TPU:8 now
where the time goes in v2:
time: 73.3 us; the launch traced here: 73 us
  blocking collectives  63.4 us (86%)
  Pallas kernels  5.99 us (8%)
  other arithmetic  1.23 us (2%)
  matrix products  0.82 us (1%)
  local copies, waits for them, and re-layouts  0.8 us (1%)
  between operations  0.76 us (1%)
    all_to_all x1, blocking collectives, shards(): lax.all_to_all(message, 'col', 0, 0, axis_index_groups=rest)  30.8 us
    all_to_all x1, blocking collectives, shards(): lax.all_to_all(message.astype(jnp.float16), 'col', 0, 0, axis_index_group...  16.4 us
    all_to_all x1, blocking collectives, shards(): lax.all_to_all(spread, 'row', 0, 0)  16.2 us
    pallas_call x1, Pallas kernels, shards(): pl.pallas_call(functools.partial(product_kernel, (ways, depth, share, row...  5.99 us

profile of v2, /device:TPU:8, one launch (start us, length us, event | category | flops | bytes accessed | tf_op | source)
XLA Modules:
  0.0 73.0 jit_solution(5868888384943401433)
XLA Ops:
  0.0 0.0 copy-start
  0.7 0.7 compare_select_fusion.spot_ref
  1.4 0.8 %broadcast_in_dim.36 = bf16[16,96,128]{2,1,0:T(8,128)(2,1)S(1)} broadcast(bf16[96,128]{1,0:T(8,128)(2,1)} %param.7), dimensions={1,2} | broadcast | bytes 417792 | tf_op jit(solution)/shard_map/broadcast_in_dim | solution.py:92
  2.2 16.2 %all_to_all.15 = bf16[16,96,128]{2,1,0:T(8,128)(2,1)S(1)} all-to-all(bf16[16,96,128]{2,1,0:T(8,128)(2,1)S(1)} %broadcast_in_dim.36), channel_id=1, replica_groups=mesh['row'=16,'col'=32] {'row'}, dimensions={0} | all-to-all | bytes 786432 | tf_op jit(solution)/shard_map/all_to_all | solution.py:97
  18.4 6.0 %shard_map.73 = f32[4,776,128]{2,1,0:T(8,128)S(1)} custom-call(s32[128]{0:T(128)S(1)} %compare_select_fusion.spot_ref, bf16[1,1,128,128,128]{4,3,2,1,0:T(8,128)(2,1)} %tiles_ref.1, bf16[1536,128]{1,0:T(8,128)(2,1)S(1)} %bitcast.9), custom_call_target="tpu_custom_call" | custom-call | tf_op jit(solution)/shard_map/pallas_call | solution.py:100
  24.4 0.1 convert_element_type.19
  24.5 16.4 %all_to_all.16 = f16[4,776,128]{2,1,0:T(8,128)(2,1)S(1)} all-to-all(f16[4,776,128]{2,1,0:T(8,128)(2,1)S(1)} %convert_element_type.19), channel_id=1, replica_groups={{0,1,16,17},{2,3,18,19},{4,5,20,21},{6,7,22,23},{8,9,24,25},{10,11,26,2..., dimensions={0} | all-to-all | bytes 1589248 | tf_op jit(solution)/shard_map/all_to_all | solution.py:114
  40.9 0.1 convert_element_type.20
  41.0 0.0 copy-start.1
  41.0 0.1 fusion
  41.1 0.2 multiply_convert_fusion
  41.3 30.8 %all_to_all.17 = f16[8,96,128]{2,1,0:T(8,128)(2,1)S(1)} all-to-all(f16[8,96,128]{2,1,0:T(8,128)(2,1)S(1)} %bitcast.10), channel_id=1, replica_groups={{0,2,4,6,8,10,12,14},{1,3,5,7,9,11,13,15},{16,18,20,22,24,26,28,30},{17..., dimensions={0} | all-to-all | bytes 393216 | tf_op jit(solution)/shard_map/all_to_all | solution.py:121
  72.1 0.1 fusion.3
  72.2 0.0 copy-done
  72.2 0.0 copy-done.1
  72.2 0.8 %fusion.2 = bf16[96,256]{1,0:T(8,128)(2,1)} fusion(bf16[128,256]{1,0:T(8,128)(2,1)S(1)} %copy-done, f32[256]{0:T(256)S(1)} %copy-done.1, f32[96,128]{1,0:T(8,128)S(1)} %fusion.3), kind=kOutput, calls=%fused_computation.4 | convolution fusion | flops 37834752 | bytes 164864 | tf_op jit(solution)/shard_map/dot_general | solution.py:124
  (1 shorter events, 0.0 us)
Async XLA Ops:
  0.0 72.2 %copy-start = (bf16[128,256]{1,0:T(8,128)(2,1)S(1)}, bf16[128,256]{1,0:T(8,128)(2,1)}, u32[]{:S(2)}) copy-start(bf16[128,256]{1,0:T(8,128)(2,1)} %param.8) | copy-start | bytes 196612
  41.0 31.2 %copy-start.1 = (f32[256]{0:T(256)S(1)}, f32[256]{0:T(256)}, u32[]{:S(2)}) copy-start(f32[256]{0:T(256)} %param.9) | copy-start | bytes 3076

commit v3 on v2

--- a/solution.py
+++ b/solution.py
@@ -26,32 +26,23 @@
     return value
 
 
-def product_kernel(parts, base, spot_ref, tiles_ref, x_ref, out_ref, place_ref, held, sems):
+def spread_kernel(features_ref, tiles_ref, spread_ref):
+    for k in range(spread_ref.shape[0]):
+        spread_ref[k] = features_ref[...]
+
+
+def product_kernel(parts, base, spot_ref, tiles_ref, x_ref, out_ref, place_ref):
     ways, depth, share, row_tiles, col_tiles = parts
-    slots, tile, _ = held.shape
-    chunks = sems.shape[0]
-    per = slots // chunks
-
-    def fetch(g):
-        span = pl.ds(g * per, per)
-        return pltpu.make_async_copy(tiles_ref.at[0, 0, span], held.at[span], sems.at[g])
-
-    for g in range(chunks):
-        fetch(g).start()
+    _, _, slots, tile, _ = tiles_ref.shape
     near = ways // 2
-    spots = row_tiles * col_tiles
-
-    for p in range(spots):
+    for p in range(row_tiles * col_tiles):
         place_ref[p] = slots
     for s in range(slots):
-        place_ref[spot_ref[s]] = s
-
-    for g in range(chunks):
-        fetch(g).wait()
+        place_ref[spot_ref[0, s]] = s
 
     def piece(p, lo, hi):
         slot = place_ref[p]
-        rows = held[jnp.minimum(slot, slots - 1), lo:hi, :]
+        rows = tiles_ref[0, 0, jnp.minimum(slot, slots - 1), lo:hi, :]
         return jnp.where(slot < slots, rows, jnp.zeros_like(rows))
 
     for d in range(ways * depth):
@@ -89,10 +80,18 @@
     ways = 2 * near
     depth = n_col // ways
 
-    spread = jnp.broadcast_to(features[None], (n_row,) + features.shape)
     row_tiles, col_tiles = total_rows // tile, n_row * share // tile
     used = jnp.arange(tile_rows.shape[2], dtype=jnp.int32) < tile_count[0, 0]
-    spots = jnp.where(used, tile_rows[0, 0] * col_tiles + tile_cols[0, 0], row_tiles * col_tiles)
+    spots = jnp.where(used, tile_rows[0] * col_tiles + tile_cols[0], row_tiles * col_tiles)
+    slots = tile_rows.shape[2]
+    smem, vmem = pl.BlockSpec(memory_space=pltpu.SMEM), pl.BlockSpec(memory_space=pltpu.VMEM)
+    spread = pl.pallas_call(
+        spread_kernel,
+        out_shape=jax.ShapeDtypeStruct((n_row,) + features.shape, features.dtype),
+        in_specs=[vmem, pl.BlockSpec(memory_space=pltpu.HBM)],
+        out_specs=vmem,
+        compiler_params=pltpu.CompilerParams(vmem_limit_bytes=50 * 2**20),
+    )(features, tile_values)
     spread, spots = lax.optimization_barrier((spread, spots))
     gathered = lax.all_to_all(spread, "row", 0, 0).reshape(n_row * features.shape[0], width)
 
@@ -100,14 +99,10 @@
     message = pl.pallas_call(
         functools.partial(product_kernel, (ways, depth, share, row_tiles, col_tiles), base),
         out_shape=jax.ShapeDtypeStruct((ways, depth * share + depth, width), jnp.float32),
-        in_specs=[pl.BlockSpec(memory_space=m) for m in (pltpu.SMEM, pltpu.HBM, pltpu.VMEM)],
-        out_specs=pl.BlockSpec(memory_space=pltpu.VMEM),
-        scratch_shapes=[
-            pltpu.SMEM((row_tiles * col_tiles + 8,), jnp.int32),
-            pltpu.VMEM(tile_values.shape[2:], tile_values.dtype),
-            pltpu.SemaphoreType.DMA((8,)),
-        ],
-        compiler_params=pltpu.CompilerParams(vmem_limit_bytes=50 * 2**20),
+        in_specs=[smem, vmem, vmem],
+        out_specs=vmem,
+        scratch_shapes=[pltpu.SMEM((row_tiles * col_tiles + 8,), jnp.int32)],
+        compiler_params=pltpu.CompilerParams(vmem_limit_bytes=12 * 2**20),
     )(spots, tile_values, gathered)
 
     pairs = [[h * half + p * near + q for h in range(2) for q in range(near)] for p in range(depth)]

time: 73.3 us -> 71.3 us (0.973)
  Pallas kernels: 5.99 us -> 4.05 us
    pallas_call x1, Pallas kernels: 5.99 us -> 4 us  [shards(): pl.pallas_call(functools.partial(product_kernel, (ways, depth, share, row...]
    unnamed x4 -> x12, local copies, waits for them, and re-layouts: 0.01 us -> 1.36 us
    broadcast_in_dim x1 -> x0, local copies, waits for them, and re-layouts: 0.79 us -> none  [shards(): spread = jnp.broadcast_to(features[None], (n_row,) + features.shape)]
where the time goes in v3:
time: 71.3 us; the launch traced here: 71.1 us
  blocking collectives  63.5 us (89%)
  Pallas kernels  4.05 us (6%)
  local copies, waits for them, and re-layouts  1.36 us (2%)
  matrix products  0.82 us (1%)
  between operations  0.77 us (1%)
    all_to_all x1, blocking collectives, shards(): lax.all_to_all(message, 'col', 0, 0, axis_index_groups=rest)  30.8 us
    all_to_all x1, blocking collectives, shards(): lax.all_to_all(message.astype(jnp.float16), 'col', 0, 0, axis_index_group...  16.4 us
    all_to_all x1, blocking collectives, shards(): lax.all_to_all(spread, 'row', 0, 0)  16.3 us
    pallas_call x1, Pallas kernels, shards(): pl.pallas_call(functools.partial(product_kernel, (ways, depth, share, row...  4 us

profile of v3, /device:TPU:8, one launch (start us, length us, event | category | flops | bytes accessed | tf_op | source)
XLA Modules:
  0.0 71.1 jit_solution(6959032473167836594)
XLA Ops:
  0.0 0.0 copy-start
  0.7 0.0 copy-start.2
  0.7 0.7 %copy-done.2 = bf16[96,128]{1,0:T(8,128)(2,1)S(1)} copy-done((bf16[96,128]{1,0:T(8,128)(2,1)S(1)}, bf16[96,128]{1,0:T(8,128)(2,1)}, u32[]{:S(2)}) %copy-start.2) | copy-done | bytes 24600
  1.4 0.0 copy-start.4
  1.4 0.0 copy-start.5
  1.4 0.0 copy-start.1
  1.4 0.1 shard_map.73
  1.5 0.6 copy-done.4
  2.1 0.0 copy-done.5
  2.1 16.3 %all_to_all.15 = bf16[16,96,128]{2,1,0:T(8,128)(2,1)S(1)} all-to-all(bf16[16,96,128]{2,1,0:T(8,128)(2,1)S(1)} %shard_map.73), channel_id=1, replica_groups=mesh['row'=16,'col'=32] {'row'}, dimensions={0} | all-to-all | bytes 786432 | tf_op jit(solution)/shard_map/all_to_all | solution.py:96
  18.4 0.0 copy-done.1
  18.4 4.0 %shard_map.74 = f32[4,776,128]{2,1,0:T(8,128)S(1)} custom-call(s32[1,128]{1,0:T(1,128)S(1)} %compare_select_fusion.spot_ref, bf16[1,1,128,128,128]{4,3,2,1,0:T(8,128)(2,1)S(1)} %copy-done.1, bf16[1536,128]{1,0:T(8,128)(2,1)S(1)} %bitcast.9), custom_call_target="tpu_custom_call" | custom-call | tf_op jit(solution)/shard_map/pallas_call | solution.py:99
  22.4 0.1 convert_element_type.19
  22.5 16.4 %all_to_all.16 = f16[4,776,128]{2,1,0:T(8,128)(2,1)S(1)} all-to-all(f16[4,776,128]{2,1,0:T(8,128)(2,1)S(1)} %convert_element_type.19), channel_id=1, replica_groups={{0,1,16,17},{2,3,18,19},{4,5,20,21},{6,7,22,23},{8,9,24,25},{10,11,26,2..., dimensions={0} | all-to-all | bytes 1589248 | tf_op jit(solution)/shard_map/all_to_all | solution.py:109
  39.0 0.1 convert_element_type.20
  39.1 0.0 copy-start.3
  39.1 0.1 fusion
  39.2 0.2 multiply_convert_fusion
  39.4 30.8 %all_to_all.17 = f16[8,96,128]{2,1,0:T(8,128)(2,1)S(1)} all-to-all(f16[8,96,128]{2,1,0:T(8,128)(2,1)S(1)} %bitcast.10), channel_id=1, replica_groups={{0,2,4,6,8,10,12,14},{1,3,5,7,9,11,13,15},{16,18,20,22,24,26,28,30},{17..., dimensions={0} | all-to-all | bytes 393216 | tf_op jit(solution)/shard_map/all_to_all | solution.py:116
  70.2 0.1 fusion.3
  70.2 0.0 copy-done
  70.2 0.0 copy-done.3
  70.2 0.8 %fusion.2 = bf16[96,256]{1,0:T(8,128)(2,1)} fusion(bf16[128,256]{1,0:T(8,128)(2,1)S(1)} %copy-done, f32[256]{0:T(256)S(1)} %copy-done.3, f32[96,128]{1,0:T(8,128)S(1)} %fusion.3), kind=kOutput, calls=%fused_computation.4 | convolution fusion | flops 37834752 | bytes 164864 | tf_op jit(solution)/shard_map/dot_general | solution.py:119
  (2 shorter events, 0.0 us)
Async XLA Ops:
  0.0 70.2 %copy-start = (bf16[128,256]{1,0:T(8,128)(2,1)S(1)}, bf16[128,256]{1,0:T(8,128)(2,1)}, u32[]{:S(2)}) copy-start(bf16[128,256]{1,0:T(8,128)(2,1)} %param.8) | copy-start | bytes 196612
  0.7 0.7 %copy-start.2 = (bf16[96,128]{1,0:T(8,128)(2,1)S(1)}, bf16[96,128]{1,0:T(8,128)(2,1)}, u32[]{:S(2)}) copy-start(bf16[96,128]{1,0:T(8,128)(2,1)} %features_ref.1) | copy-start | bytes 73732
  1.4 0.7 copy-start.4
  1.4 0.7 copy-start.5
  1.4 17.0 %copy-start.1 = (bf16[1,1,128,128,128]{4,3,2,1,0:T(8,128)(2,1)S(1)}, bf16[1,1,128,128,128]{4,3,2,1,0:T(8,128)(2,1)}, u32[]{:S(2)}) copy-start(bf16[1,1,128,128,128]{4,3,2,1,0:T(8,128)(2,1)} %tiles_ref.3) | copy-start | bytes 12582916
  39.1 31.2 %copy-start.3 = (f32[256]{0:T(256)S(1)}, f32[256]{0:T(256)}, u32[]{:S(2)}) copy-start(f32[256]{0:T(256)} %param.9) | copy-start | bytes 3076

commit v4 on v3

--- a/solution.py
+++ b/solution.py
@@ -81,8 +81,6 @@
     depth = n_col // ways
 
     row_tiles, col_tiles = total_rows // tile, n_row * share // tile
-    used = jnp.arange(tile_rows.shape[2], dtype=jnp.int32) < tile_count[0, 0]
-    spots = jnp.where(used, tile_rows[0] * col_tiles + tile_cols[0], row_tiles * col_tiles)
     slots = tile_rows.shape[2]
     smem, vmem = pl.BlockSpec(memory_space=pltpu.SMEM), pl.BlockSpec(memory_space=pltpu.VMEM)
     spread = pl.pallas_call(
@@ -92,8 +90,12 @@
         out_specs=vmem,
         compiler_params=pltpu.CompilerParams(vmem_limit_bytes=50 * 2**20),
     )(features, tile_values)
-    spread, spots = lax.optimization_barrier((spread, spots))
+    used = (jnp.arange(slots, dtype=jnp.int32) < tile_count[0, 0]).astype(jnp.int32)
+    spread, used = lax.optimization_barrier((spread, used))
     gathered = lax.all_to_all(spread, "row", 0, 0).reshape(n_row * features.shape[0], width)
+
+    gathered, rows, cols = lax.optimization_barrier((gathered, tile_rows[0], tile_cols[0]))
+    spots = jnp.where(used > 0, rows * col_tiles + cols, row_tiles * col_tiles)
 
     base = 7
     message = pl.pallas_call(

time: 71.3 us -> 70.9 us (level)
  no operation moved by 1% of the time
where the time goes in v4:
time: 70.9 us; the launch traced here: 70.6 us
  blocking collectives  63.7 us (90%)
  Pallas kernels  4.06 us (6%)
  matrix products  0.82 us (1%)
  between operations  0.79 us (1%)
  local copies, waits for them, and re-layouts  0.75 us (1%)
    all_to_all x1, blocking collectives, shards(): lax.all_to_all(message, 'col', 0, 0, axis_index_groups=rest)  30.8 us
    all_to_all x1, blocking collectives, shards(): lax.all_to_all(spread, 'row', 0, 0)  16.5 us
    all_to_all x1, blocking collectives, shards(): lax.all_to_all(message.astype(jnp.float16), 'col', 0, 0, axis_index_group...  16.4 us
    pallas_call x1, Pallas kernels, shards(): pl.pallas_call(functools.partial(product_kernel, (ways, depth, share, row...  4.01 us

profile of v4, /device:TPU:8, one launch (start us, length us, event | category | flops | bytes accessed | tf_op | source)
XLA Modules:
  0.0 70.6 jit_solution(10467305293575174760)
XLA Ops:
  0.0 0.0 copy-start
  0.7 0.0 copy-start.2
  0.7 0.7 %copy-done.2 = bf16[96,128]{1,0:T(8,128)(2,1)S(1)} copy-done((bf16[96,128]{1,0:T(8,128)(2,1)S(1)}, bf16[96,128]{1,0:T(8,128)(2,1)}, u32[]{:S(2)}) %copy-start.2) | copy-done | bytes 24600
  1.4 0.0 copy-start.4
  1.4 0.0 copy-start.5
  1.4 0.0 copy-start.1
  1.4 0.1 shard_map.73
  1.5 16.5 %all_to_all.15 = bf16[16,96,128]{2,1,0:T(8,128)(2,1)S(1)} all-to-all(bf16[16,96,128]{2,1,0:T(8,128)(2,1)S(1)} %shard_map.73), channel_id=1, replica_groups=mesh['row'=16,'col'=32] {'row'}, dimensions={0} | all-to-all | bytes 786432 | tf_op jit(solution)/shard_map/all_to_all | solution.py:95
  18.0 0.0 copy-done.4
  18.0 0.0 copy-done.5
  18.0 0.0 copy-done.1
  18.0 4.0 %shard_map.74 = f32[4,776,128]{2,1,0:T(8,128)S(1)} custom-call(s32[1,128]{1,0:T(1,128)S(1)} %bitcast_select_fusion.spot_ref, bf16[1,1,128,128,128]{4,3,2,1,0:T(8,128)(2,1)S(1)} %copy-done.1, bf16[1536,128]{1,0:T(8,128)(2,1)S(1)} %bitcast.11), custom_call_target="tpu_custom_call" | custom-call | tf_op jit(solution)/shard_map/pallas_call | solution.py:101
  22.0 0.1 convert_element_type.23
  22.1 16.4 %all_to_all.16 = f16[4,776,128]{2,1,0:T(8,128)(2,1)S(1)} all-to-all(f16[4,776,128]{2,1,0:T(8,128)(2,1)S(1)} %convert_element_type.23), channel_id=1, replica_groups={{0,1,16,17},{2,3,18,19},{4,5,20,21},{6,7,22,23},{8,9,24,25},{10,11,26,2..., dimensions={0} | all-to-all | bytes 1589248 | tf_op jit(solution)/shard_map/all_to_all | solution.py:111
  38.5 0.1 convert_element_type.24
  38.7 0.0 copy-start.3
  38.7 0.1 fusion
  38.8 0.2 multiply_convert_fusion
  39.0 30.8 %all_to_all.17 = f16[8,96,128]{2,1,0:T(8,128)(2,1)S(1)} all-to-all(f16[8,96,128]{2,1,0:T(8,128)(2,1)S(1)} %bitcast.12), channel_id=1, replica_groups={{0,2,4,6,8,10,12,14},{1,3,5,7,9,11,13,15},{16,18,20,22,24,26,28,30},{17..., dimensions={0} | all-to-all | bytes 393216 | tf_op jit(solution)/shard_map/all_to_all | solution.py:118
  69.7 0.1 fusion.3
  69.8 0.0 copy-done
  69.8 0.0 copy-done.3
  69.8 0.8 %fusion.2 = bf16[96,256]{1,0:T(8,128)(2,1)} fusion(bf16[128,256]{1,0:T(8,128)(2,1)S(1)} %copy-done, f32[256]{0:T(256)S(1)} %copy-done.3, f32[96,128]{1,0:T(8,128)S(1)} %fusion.3), kind=kOutput, calls=%fused_computation.4 | convolution fusion | flops 37834752 | bytes 164864 | tf_op jit(solution)/shard_map/dot_general | solution.py:121
  (3 shorter events, 0.0 us)
Async XLA Ops:
  0.0 69.8 %copy-start = (bf16[128,256]{1,0:T(8,128)(2,1)S(1)}, bf16[128,256]{1,0:T(8,128)(2,1)}, u32[]{:S(2)}) copy-start(bf16[128,256]{1,0:T(8,128)(2,1)} %param.8) | copy-start | bytes 196612
  0.7 0.7 %copy-start.2 = (bf16[96,128]{1,0:T(8,128)(2,1)S(1)}, bf16[96,128]{1,0:T(8,128)(2,1)}, u32[]{:S(2)}) copy-start(bf16[96,128]{1,0:T(8,128)(2,1)} %features_ref.1) | copy-start | bytes 73732
  1.4 16.5 %copy-start.4 = (s32[1,1,128]{2,1,0:T(1,128)S(1)}, s32[1,1,128]{2,1,0:T(1,128)}, u32[]{:S(2)}) copy-start(s32[1,1,128]{2,1,0:T(1,128)} %param.12) | copy-start | bytes 1540
  1.4 16.5 %copy-start.5 = (s32[1,1,128]{2,1,0:T(1,128)S(1)}, s32[1,1,128]{2,1,0:T(1,128)}, u32[]{:S(2)}) copy-start(s32[1,1,128]{2,1,0:T(1,128)} %param.11) | copy-start | bytes 1540
  1.4 16.5 %copy-start.1 = (bf16[1,1,128,128,128]{4,3,2,1,0:T(8,128)(2,1)S(1)}, bf16[1,1,128,128,128]{4,3,2,1,0:T(8,128)(2,1)}, u32[]{:S(2)}) copy-start(bf16[1,1,128,128,128]{4,3,2,1,0:T(8,128)(2,1)} %tiles_ref.3) | copy-start | bytes 12582916
  38.7 31.2 %copy-start.3 = (f32[256]{0:T(256)S(1)}, f32[256]{0:T(256)}, u32[]{:S(2)}) copy-start(f32[256]{0:T(256)} %param.9) | copy-start | bytes 3076

commit v5 on v4

--- a/solution.py
+++ b/solution.py
@@ -31,15 +31,10 @@
         spread_ref[k] = features_ref[...]
 
 
-def product_kernel(parts, base, spot_ref, tiles_ref, x_ref, out_ref, place_ref):
+def product_kernel(parts, base, place_ref, tiles_ref, x_ref, out_ref):
     ways, depth, share, row_tiles, col_tiles = parts
     _, _, slots, tile, _ = tiles_ref.shape
     near = ways // 2
-    for p in range(row_tiles * col_tiles):
-        place_ref[p] = slots
-    for s in range(slots):
-        place_ref[spot_ref[0, s]] = s
-
     def piece(p, lo, hi):
         slot = place_ref[p]
         rows = tiles_ref[0, 0, jnp.minimum(slot, slots - 1), lo:hi, :]
@@ -90,12 +85,16 @@
         out_specs=vmem,
         compiler_params=pltpu.CompilerParams(vmem_limit_bytes=50 * 2**20),
     )(features, tile_values)
-    used = (jnp.arange(slots, dtype=jnp.int32) < tile_count[0, 0]).astype(jnp.int32)
+    index = jnp.arange(slots, dtype=jnp.int32)
+    used = jnp.where(index < tile_count[0, 0], index - slots, 0)
     spread, used = lax.optimization_barrier((spread, used))
     gathered = lax.all_to_all(spread, "row", 0, 0).reshape(n_row * features.shape[0], width)
 
     gathered, rows, cols = lax.optimization_barrier((gathered, tile_rows[0], tile_cols[0]))
-    spots = jnp.where(used > 0, rows * col_tiles + cols, row_tiles * col_tiles)
+    spots = rows * col_tiles + cols
+
+    here = spots[0][None, :] == jnp.arange(row_tiles * col_tiles, dtype=jnp.int32)[:, None]
+    place = slots + jnp.sum(jnp.where(here, used, 0), axis=1)
 
     base = 7
     message = pl.pallas_call(
@@ -103,9 +102,8 @@
         out_shape=jax.ShapeDtypeStruct((ways, depth * share + depth, width), jnp.float32),
         in_specs=[smem, vmem, vmem],
         out_specs=vmem,
-        scratch_shapes=[pltpu.SMEM((row_tiles * col_tiles + 8,), jnp.int32)],
         compiler_params=pltpu.CompilerParams(vmem_limit_bytes=12 * 2**20),
-    )(spots, tile_values, gathered)
+    )(place, tile_values, gathered)
 
     pairs = [[h * half + p * near + q for h in range(2) for q in range(near)] for p in range(depth)]
     came = lax.all_to_all(message.astype(jnp.float16), "col", 0, 0, axis_index_groups=pairs).astype(jnp.float32)

time: 70.9 us -> 70.7 us (level)
  no operation moved by 1% of the time
where the time goes in v5:
time: 70.7 us; the launch traced here: 70.5 us
  blocking collectives  63.7 us (90%)
  Pallas kernels  3.74 us (5%)
  matrix products  0.82 us (1%)
  between operations  0.79 us (1%)
  local copies, waits for them, and re-layouts  0.75 us (1%)
  other arithmetic  0.71 us (1%)
    all_to_all x1, blocking collectives, shards(): lax.all_to_all(message, 'col', 0, 0, axis_index_groups=rest)  30.8 us
    all_to_all x1, blocking collectives, shards(): lax.all_to_all(spread, 'row', 0, 0)  16.5 us
    all_to_all x1, blocking collectives, shards(): lax.all_to_all(message.astype(jnp.float16), 'col', 0, 0, axis_index_group...  16.4 us
    pallas_call x1, Pallas kernels, shards(): pl.pallas_call(functools.partial(product_kernel, (ways, depth, share, row...  3.69 us

profile of v5, /device:TPU:8, one launch (start us, length us, event | category | flops | bytes accessed | tf_op | source)
XLA Modules:
  0.0 70.5 jit_solution(3480020729688905754)
XLA Ops:
  0.0 0.0 copy-start
  0.7 0.0 copy-start.2
  0.7 0.7 %copy-done.2 = bf16[96,128]{1,0:T(8,128)(2,1)S(1)} copy-done((bf16[96,128]{1,0:T(8,128)(2,1)S(1)}, bf16[96,128]{1,0:T(8,128)(2,1)}, u32[]{:S(2)}) %copy-start.2) | copy-done | bytes 24600
  1.4 0.0 copy-start.4
  1.4 0.0 copy-start.5
  1.4 0.0 copy-start.1
  1.4 0.1 shard_map.73
  1.5 16.5 %all_to_all.15 = bf16[16,96,128]{2,1,0:T(8,128)(2,1)S(1)} all-to-all(bf16[16,96,128]{2,1,0:T(8,128)(2,1)S(1)} %shard_map.73), channel_id=1, replica_groups=mesh['row'=16,'col'=32] {'row'}, dimensions={0} | all-to-all | bytes 786432 | tf_op jit(solution)/shard_map/all_to_all | solution.py:91
  18.0 0.0 copy-done.4
  18.0 0.0 copy-done.5
  18.0 0.1 select_reduce_fusion
  18.1 0.0 copy-done.1
  18.1 3.7 %shard_map.74 = f32[4,776,128]{2,1,0:T(8,128)S(1)} custom-call(s32[288]{0:T(512)S(1)} %broadcast_add_fusion.place_ref, bf16[1,1,128,128,128]{4,3,2,1,0:T(8,128)(2,1)S(1)} %copy-done.1, bf16[1536,128]{1,0:T(8,128)(2,1)S(1)} %bitcast.11), custom_call_target="tpu_custom_call" | custom-call | tf_op jit(solution)/shard_map/pallas_call | solution.py:100
  21.8 0.1 convert_element_type.19
  22.0 16.4 %all_to_all.16 = f16[4,776,128]{2,1,0:T(8,128)(2,1)S(1)} all-to-all(f16[4,776,128]{2,1,0:T(8,128)(2,1)S(1)} %convert_element_type.19), channel_id=1, replica_groups={{0,1,16,17},{2,3,18,19},{4,5,20,21},{6,7,22,23},{8,9,24,25},{10,11,26,2..., dimensions={0} | all-to-all | bytes 1589248 | tf_op jit(solution)/shard_map/all_to_all | solution.py:109
  38.4 0.1 convert_element_type.20
  38.5 0.0 copy-start.3
  38.5 0.1 fusion
  38.6 0.2 multiply_convert_fusion
  38.8 30.8 %all_to_all.17 = f16[8,96,128]{2,1,0:T(8,128)(2,1)S(1)} all-to-all(f16[8,96,128]{2,1,0:T(8,128)(2,1)S(1)} %bitcast.12), channel_id=1, replica_groups={{0,2,4,6,8,10,12,14},{1,3,5,7,9,11,13,15},{16,18,20,22,24,26,28,30},{17..., dimensions={0} | all-to-all | bytes 393216 | tf_op jit(solution)/shard_map/all_to_all | solution.py:116
  69.6 0.1 fusion.3
  69.6 0.0 copy-done
  69.7 0.0 copy-done.3
  69.7 0.8 %fusion.2 = bf16[96,256]{1,0:T(8,128)(2,1)} fusion(bf16[128,256]{1,0:T(8,128)(2,1)S(1)} %copy-done, f32[256]{0:T(256)S(1)} %copy-done.3, f32[96,128]{1,0:T(8,128)S(1)} %fusion.3), kind=kOutput, calls=%fused_computation.4 | convolution fusion | flops 37834752 | bytes 164864 | tf_op jit(solution)/shard_map/dot_general | solution.py:119
  (4 shorter events, 0.0 us)
Async XLA Ops:
  0.0 69.6 %copy-start = (bf16[128,256]{1,0:T(8,128)(2,1)S(1)}, bf16[128,256]{1,0:T(8,128)(2,1)}, u32[]{:S(2)}) copy-start(bf16[128,256]{1,0:T(8,128)(2,1)} %param.8) | copy-start | bytes 196612
  0.7 0.7 %copy-start.2 = (bf16[96,128]{1,0:T(8,128)(2,1)S(1)}, bf16[96,128]{1,0:T(8,128)(2,1)}, u32[]{:S(2)}) copy-start(bf16[96,128]{1,0:T(8,128)(2,1)} %features_ref.1) | copy-start | bytes 73732
  1.4 16.5 %copy-start.4 = (s32[1,1,128]{2,1,0:T(1,128)S(1)}, s32[1,1,128]{2,1,0:T(1,128)}, u32[]{:S(2)}) copy-start(s32[1,1,128]{2,1,0:T(1,128)} %param.12) | copy-start | bytes 1540
  1.4 16.5 %copy-start.5 = (s32[1,1,128]{2,1,0:T(1,128)S(1)}, s32[1,1,128]{2,1,0:T(1,128)}, u32[]{:S(2)}) copy-start(s32[1,1,128]{2,1,0:T(1,128)} %param.11) | copy-start | bytes 1540
  1.4 16.7 %copy-start.1 = (bf16[1,1,128,128,128]{4,3,2,1,0:T(8,128)(2,1)S(1)}, bf16[1,1,128,128,128]{4,3,2,1,0:T(8,128)(2,1)}, u32[]{:S(2)}) copy-start(bf16[1,1,128,128,128]{4,3,2,1,0:T(8,128)(2,1)} %tiles_ref.3) | copy-start | bytes 12582916
  38.5 31.2 %copy-start.3 = (f32[256]{0:T(256)S(1)}, f32[256]{0:T(256)}, u32[]{:S(2)}) copy-start(f32[256]{0:T(256)} %param.9) | copy-start | bytes 3076

commit v6 on v5

--- a/solution.py
+++ b/solution.py
@@ -14,9 +14,12 @@
 
 def level_of(peak, base):
     level = jnp.zeros(peak.shape, jnp.float32)
+    scale = jnp.ones(peak.shape, jnp.float32)
     for k in range(1, LEVELS + 1):
-        level = level + jnp.where(peak < 2.0 ** (15 - base - STEP * k), 1.0, 0.0)
-    return level
+        small = peak < 2.0 ** (15 - base - STEP * k)
+        level = jnp.where(small, float(k), level)
+        scale = jnp.where(small, 2.0 ** (STEP * k), scale)
+    return level, scale
 
 
 def power(level, sign):
@@ -59,8 +62,8 @@
                 x_ref[j * tile : (j + 2) * tile, :],
                 preferred_element_type=jnp.float32,
             )
-        level = level_of(jnp.max(jnp.abs(value), axis=0, keepdims=True), base)
-        out_ref[way, at * share : (at + 1) * share, :] = value * (power(level, 1) * 2.0**base)
+        level, scale = level_of(jnp.max(jnp.abs(value), axis=0, keepdims=True), base)
+        out_ref[way, at * share : (at + 1) * share, :] = value * (scale * 2.0**base)
         out_ref[way, depth * share + at : depth * share + at + 1, :] = level
 
 

time: 70.7 us -> 70.7 us (level)
  no operation moved by 1% of the time
where the time goes in v6:
time: 70.7 us; the launch traced here: 70.4 us
  blocking collectives  63.7 us (90%)
  Pallas kernels  3.69 us (5%)
  matrix products  0.82 us (1%)
  between operations  0.79 us (1%)
  local copies, waits for them, and re-layouts  0.75 us (1%)
  other arithmetic  0.71 us (1%)
    all_to_all x1, blocking collectives, shards(): lax.all_to_all(message, 'col', 0, 0, axis_index_groups=rest)  30.8 us
    all_to_all x1, blocking collectives, shards(): lax.all_to_all(spread, 'row', 0, 0)  16.5 us
    all_to_all x1, blocking collectives, shards(): lax.all_to_all(message.astype(jnp.float16), 'col', 0, 0, axis_index_group...  16.4 us
    pallas_call x1, Pallas kernels, shards(): pl.pallas_call(functools.partial(product_kernel, (ways, depth, share, row...  3.63 us

profile of v6, /device:TPU:8, one launch (start us, length us, event | category | flops | bytes accessed | tf_op | source)
XLA Modules:
  0.0 70.4 jit_solution(9587842791175382832)
XLA Ops:
  0.0 0.0 copy-start
  0.7 0.0 copy-start.2
  0.7 0.7 %copy-done.2 = bf16[96,128]{1,0:T(8,128)(2,1)S(1)} copy-done((bf16[96,128]{1,0:T(8,128)(2,1)S(1)}, bf16[96,128]{1,0:T(8,128)(2,1)}, u32[]{:S(2)}) %copy-start.2) | copy-done | bytes 24600
  1.4 0.0 copy-start.4
  1.4 0.0 copy-start.5
  1.4 0.0 copy-start.1
  1.4 0.1 shard_map.73
  1.5 16.5 %all_to_all.15 = bf16[16,96,128]{2,1,0:T(8,128)(2,1)S(1)} all-to-all(bf16[16,96,128]{2,1,0:T(8,128)(2,1)S(1)} %shard_map.73), channel_id=1, replica_groups=mesh['row'=16,'col'=32] {'row'}, dimensions={0} | all-to-all | bytes 786432 | tf_op jit(solution)/shard_map/all_to_all | solution.py:94
  18.0 0.0 copy-done.4
  18.0 0.0 copy-done.5
  18.0 0.1 select_reduce_fusion
  18.1 0.0 copy-done.1
  18.1 3.6 %shard_map.74 = f32[4,776,128]{2,1,0:T(8,128)S(1)} custom-call(s32[288]{0:T(512)S(1)} %broadcast_add_fusion.place_ref, bf16[1,1,128,128,128]{4,3,2,1,0:T(8,128)(2,1)S(1)} %copy-done.1, bf16[1536,128]{1,0:T(8,128)(2,1)S(1)} %bitcast.11), custom_call_target="tpu_custom_call" | custom-call | tf_op jit(solution)/shard_map/pallas_call | solution.py:103
  21.8 0.1 convert_element_type.19
  21.9 16.4 %all_to_all.16 = f16[4,776,128]{2,1,0:T(8,128)(2,1)S(1)} all-to-all(f16[4,776,128]{2,1,0:T(8,128)(2,1)S(1)} %convert_element_type.19), channel_id=1, replica_groups={{0,1,16,17},{2,3,18,19},{4,5,20,21},{6,7,22,23},{8,9,24,25},{10,11,26,2..., dimensions={0} | all-to-all | bytes 1589248 | tf_op jit(solution)/shard_map/all_to_all | solution.py:112
  38.3 0.1 convert_element_type.20
  38.4 0.0 copy-start.3
  38.4 0.1 fusion
  38.6 0.2 multiply_convert_fusion
  38.7 30.8 %all_to_all.17 = f16[8,96,128]{2,1,0:T(8,128)(2,1)S(1)} all-to-all(f16[8,96,128]{2,1,0:T(8,128)(2,1)S(1)} %bitcast.12), channel_id=1, replica_groups={{0,2,4,6,8,10,12,14},{1,3,5,7,9,11,13,15},{16,18,20,22,24,26,28,30},{17..., dimensions={0} | all-to-all | bytes 393216 | tf_op jit(solution)/shard_map/all_to_all | solution.py:119
  69.5 0.1 fusion.3
  69.6 0.0 copy-done
  69.6 0.0 copy-done.3
  69.6 0.8 %fusion.2 = bf16[96,256]{1,0:T(8,128)(2,1)} fusion(bf16[128,256]{1,0:T(8,128)(2,1)S(1)} %copy-done, f32[256]{0:T(256)S(1)} %copy-done.3, f32[96,128]{1,0:T(8,128)S(1)} %fusion.3), kind=kOutput, calls=%fused_computation.4 | convolution fusion | flops 37834752 | bytes 164864 | tf_op jit(solution)/shard_map/dot_general | solution.py:122
  (4 shorter events, 0.0 us)
Async XLA Ops:
  0.0 69.6 %copy-start = (bf16[128,256]{1,0:T(8,128)(2,1)S(1)}, bf16[128,256]{1,0:T(8,128)(2,1)}, u32[]{:S(2)}) copy-start(bf16[128,256]{1,0:T(8,128)(2,1)} %param.8) | copy-start | bytes 196612
  0.7 0.7 %copy-start.2 = (bf16[96,128]{1,0:T(8,128)(2,1)S(1)}, bf16[96,128]{1,0:T(8,128)(2,1)}, u32[]{:S(2)}) copy-start(bf16[96,128]{1,0:T(8,128)(2,1)} %features_ref.1) | copy-start | bytes 73732
  1.4 16.5 %copy-start.4 = (s32[1,1,128]{2,1,0:T(1,128)S(1)}, s32[1,1,128]{2,1,0:T(1,128)}, u32[]{:S(2)}) copy-start(s32[1,1,128]{2,1,0:T(1,128)} %param.12) | copy-start | bytes 1540
  1.4 16.5 %copy-start.5 = (s32[1,1,128]{2,1,0:T(1,128)S(1)}, s32[1,1,128]{2,1,0:T(1,128)}, u32[]{:S(2)}) copy-start(s32[1,1,128]{2,1,0:T(1,128)} %param.11) | copy-start | bytes 1540
  1.4 16.7 %copy-start.1 = (bf16[1,1,128,128,128]{4,3,2,1,0:T(8,128)(2,1)S(1)}, bf16[1,1,128,128,128]{4,3,2,1,0:T(8,128)(2,1)}, u32[]{:S(2)}) copy-start(bf16[1,1,128,128,128]{4,3,2,1,0:T(8,128)(2,1)} %tiles_ref.3) | copy-start | bytes 12582916
  38.4 31.2 %copy-start.3 = (f32[256]{0:T(256)S(1)}, f32[256]{0:T(256)}, u32[]{:S(2)}) copy-start(f32[256]{0:T(256)} %param.9) | copy-start | bytes 3076
